TPU v7x, 256 devices: a whole 4x4x8 slice. The times are simulated.
256 devices in a mesh: tok: 16 (over x, y_hi, core), col: 8 (over z), grp: 2 (over y_lo).
Axes of the slice: x: 4, y: 4 (y_hi: 2, y_lo: 2; y = y_hi * 2 + y_lo), z: 8, core: 2. Of those that a mesh axis runs over, the one named last changes fastest.
Arguments:
- calibration: bfloat16 [24576, 4096], P(('tok', 'grp'), 'col'), may hold values from -1.1 to 1.1
- weight: float32 [4096, 4096], P(('tok', 'grp'), 'col'), may hold values from -6 to 6
- tile_mask: int32 [32, 32], P(('tok', 'grp'), 'col'), may hold values 0 or 1
- token_ids: int32 [2048], P(('tok', 'grp')), may hold values from 0 to 767
Outputs:
- new_weight: bfloat16 [4096, 4096], P(('tok', 'grp'), 'col')
- outputs: bfloat16 [2048, 4096], P('col', ('tok', 'grp'))
All inputs are finite; a program needn't handle non-finite values. No bound on the sum of `tile_mask` on one device may be relied on, other than what follows from the above.
Results may differ from a plain program's by a relative error of at most 0.0019.
The roundings to bfloat16 on the way count: a program that leaves them out, or rounds other values in their place, can miss the bound.
Values may be sent and summed in bfloat16 or wider, within the bound.
No kernel may reach another device: no remote copies, remote signals or barrier semaphores. Data moves between devices by JAX's collectives and lax.ppermute only.
A program may use at most 64 MiB of HBM per device.

v0:
```python
import jax
import jax.numpy as jnp
from jax import lax
from jax.sharding import PartitionSpec as P

TILE = 128
ITERS = 3
DAMPING = 0.1


def expand_tiles(tile_flags):
    tile_rows, tile_cols = tile_flags.shape
    expanded = jnp.broadcast_to(
        tile_flags.astype(jnp.float32)[:, None, :, None], (tile_rows, TILE, tile_cols, TILE)
    )
    return expanded.reshape(tile_rows * TILE, tile_cols * TILE)


def per_device(calibration, weight, tile_mask, token_ids):
    col_width = calibration.shape[1]
    col_count = lax.axis_size("col")
    width = col_width * col_count
    col_place = lax.axis_index("col")
    squares = jnp.sum(jnp.square(calibration.astype(jnp.float32)))
    trace_total = lax.psum(squares, ("tok", "col", "grp"))
    partial_gram = lax.dot_general(
        calibration,
        lax.all_gather(calibration, "col", axis=1, tiled=True),
        (((0,), (0,)), ((), ())),
        preferred_element_type=jnp.float32,
    )
    gram_slice = lax.psum_scatter(partial_gram, ("tok", "grp"), scatter_dimension=1, tiled=True)
    gram_rows = lax.all_gather(gram_slice, ("tok", "grp"), axis=1, tiled=True)
    trace_scale = trace_total / width
    row_ids = col_place * col_width + lax.broadcasted_iota(jnp.int32, gram_rows.shape, 0)
    col_ids = lax.broadcasted_iota(jnp.int32, gram_rows.shape, 1)
    stationary = gram_rows / trace_scale + jnp.where(row_ids == col_ids, DAMPING, 0.0)

    def apply_gram(operand):
        return lax.dot_general(
            lax.all_gather(operand, "col", axis=1, tiled=True),
            stationary,
            (((1,), (1,)), ((), ())),
            precision=lax.Precision.HIGHEST,
            preferred_element_type=jnp.float32,
        )

    keep_mask = expand_tiles(tile_mask)
    current = weight * keep_mask
    residual = apply_gram(current - weight)
    for iteration in range(ITERS):
        gradient = residual * keep_mask
        image_rows = apply_gram(gradient)
        sums_pair = lax.psum(
            (jnp.sum(gradient * gradient), jnp.sum(gradient * image_rows)), ("tok", "col", "grp")
        )
        length = sums_pair[0] / sums_pair[1]
        current = current - length * gradient
        if iteration + 1 < ITERS:
            residual = residual - length * image_rows
    new_weight = current.astype(jnp.bfloat16)
    chosen = jnp.take(calibration, token_ids, axis=0)
    all_chosen = lax.all_gather(chosen, ("tok", "grp"), axis=0, tiled=True)
    outputs = lax.psum_scatter(
        lax.dot_general(
            all_chosen, new_weight, (((1,), (1,)), ((), ())), preferred_element_type=jnp.float32
        ),
        "col",
        scatter_dimension=0,
        tiled=True,
    )
    return (new_weight, outputs.astype(jnp.bfloat16))


def solution(mesh):
    placed = (
        P(("tok", "grp"), "col"),
        P(("tok", "grp"), "col"),
        P(("tok", "grp"), "col"),
        P(("tok", "grp")),
    )
    return jax.shard_map(
        per_device,
        mesh=mesh,
        in_specs=placed,
        out_specs=(P(("tok", "grp"), "col"), P("col", ("tok", "grp"))),
        check_vma=False,
    )
```

profile of v0, /device:TPU:2, one launch (start us, length us, event | category | flops | bytes accessed | tf_op | source)
XLA Modules:
  0.0 833.4 jit_solution(12873526358352657317)
XLA Ops:
  7.9 79.3 %all-gather.10.cloned.1.call-done = bf16[768,4096]{1,0:T(8,128)(2,1)} async-done(((bf16[768,512]{1,0:T(8,128)(2,1)}), bf16[768,4096]{1,0:T(8,128)(2,1)}) %all-gather.10.cloned.1.call-update) | async-done | bytes 6291472 | tf_op jit(solution)/shard_map/all_gather | solution.py:28
  87.3 9.7 %fusion.4 = f32[512,4096]{1,0:T(8,128)} fusion(bf16[768,512]{1,0:T(8,128)(2,1)} %param.4, bf16[768,4096]{1,0:T(8,128)(2,1)} %all-gather.10.cloned.1.call-done), kind=kOutput, calls=%fused_computation.27 | convolution fusion | flops 3221225472 | bytes 15466496 | tf_op jit(solution)/shard_map/dot_general | solution.py:26
  97.1 143.3 %reduce-scatter.3.cloned.1.call-done = f32[512,128]{1,0:T(8,128)} async-done(((f32[512,4096]{1,0:T(8,128)}), f32[512,128]{1,0:T(8,128)}) %reduce-scatter.3.cloned.1.call-update) | async-done | bytes 262160 | tf_op jit(solution)/shard_map/reduce_scatter | solution.py:32
  240.6 0.7 multiply_subtract_fusion.1
  241.4 1.0 multiply_reduce_fusion
  242.4 77.8 %psum.49 = f32[]{:T(128)} all-reduce(f32[]{:T(128)} %multiply_reduce_fusion), channel_id=1, replica_groups=mesh['tok'=16,'col'=8,'grp'=2] {'tok','col','grp'}, use_global_device_ids=true, to_apply=%region_2.0 | all-reduce | flops 1 | bytes 8 | tf_op jit(solution)/shard_map/psum | solution.py:25
  320.8 22.7 %all-gather.12.cloned.1.call-done = f32[512,4096]{1,0:T(8,128)} async-done(((f32[512,128]{1,0:T(8,128)}), f32[512,4096]{1,0:T(8,128)}) %all-gather.12.cloned.1.call-update) | async-done | bytes 8388624 | tf_op jit(solution)/shard_map/all_gather | solution.py:33
  343.5 6.3 select_add_fusion
  349.8 36.7 %all-gather.8.cloned.1.call-done = f32[128,4096]{1,0:T(8,128)} async-done(((f32[128,512]{1,0:T(8,128)}), f32[128,4096]{1,0:T(8,128)}) %all-gather.8.cloned.1.call-update) | async-done | bytes 2097168 | tf_op jit(solution)/shard_map/all_gather | solution.py:41
  386.5 13.5 %broadcast_multiply_fusion.1 = (f32[128,512]{1,0:T(8,128)}, f32[128,512]{1,0:T(8,128)S(1)}) fusion(f32[512]{0:T(512)S(1)} %broadcast_bitcast_fusion, f32[128,4096]{1,0:T(8,128)} %all-gather.8.cloned.1.call-done, f32[512,4096]{1,0:T(8,128)} %select_add_fusion), kind=kOutput, calls=%fused_computation.19 | convolution fusion | flops 3221291008 | bytes 11012096 | tf_op jit(solution)/shard_map/dot_general | solution.py:40
  400.6 39.3 %all-gather.14.cloned.1.call-done = f32[128,4096]{1,0:T(8,128)} async-done(((f32[128,512]{1,0:T(8,128)}), f32[128,4096]{1,0:T(8,128)}) %all-gather.14.cloned.1.call-update) | async-done | bytes 2097168 | tf_op jit(solution)/shard_map/all_gather | solution.py:41
  439.8 13.4 %multiply_reduce_fusion.4 = (f32[]{:T(128)}, f32[]{:T(128)}, f32[128,512]{1,0:T(8,128)S(1)}) fusion(f32[128,512]{1,0:T(8,128)} %get-tuple-element.14, f32[128,4096]{1,0:T(8,128)} %all-gather.14.cloned.1.call-done, f32[512,4096]{1,0:T(8,128)} %select_add_fusion), kind=kOutput, calls=%fused_computation.16 | convolution fusion | flops 3221487616 | bytes 11010056 | tf_op jit(solution)/shard_map/dot_general | solution.py:40
  453.2 74.2 %all-reduce.2 = (f32[]{:T(128)}, f32[]{:T(128)}) all-reduce(f32[]{:T(128)} %get-tuple-element.5, f32[]{:T(128)} %get-tuple-element.4), channel_id=1, replica_groups=mesh['tok'=16,'col'=8,'grp'=2] {'tok','col','grp'}, use_global_device_ids=true, to_apply=%region_4.5 | all-reduce | flops 2 | bytes 16 | tf_op jit(solution)/shard_map/psum | solution.py:54
  528.7 0.8 broadcast_multiply_fusion
  529.8 37.6 %all-gather.16.cloned.1.call-done = f32[128,4096]{1,0:T(8,128)} async-done(((f32[128,512]{1,0:T(8,128)}), f32[128,4096]{1,0:T(8,128)}) %all-gather.16.cloned.1.call-update) | async-done | bytes 2097168 | tf_op jit(solution)/shard_map/all_gather | solution.py:41
  567.4 13.4 %multiply_reduce_fusion.2 = (f32[]{:T(128)}, f32[]{:T(128)}, f32[128,512]{1,0:T(8,128)S(1)}) fusion(f32[128,512]{1,0:T(8,128)} %broadcast_multiply_fusion, f32[128,4096]{1,0:T(8,128)} %all-gather.16.cloned.1.call-done, f32[512,4096]{1,0:T(8,128)} %select_add_fusion), kind=kOutput, calls=%fused_computation.13 | convolution fusion | flops 3221487616 | bytes 11010056 | tf_op jit(solution)/shard_map/dot_general | solution.py:40
  580.8 74.2 %all-reduce.1 = (f32[]{:T(128)}, f32[]{:T(128)}) all-reduce(f32[]{:T(128)} %get-tuple-element.3, f32[]{:T(128)} %get-tuple-element.2), channel_id=1, replica_groups=mesh['tok'=16,'col'=8,'grp'=2] {'tok','col','grp'}, use_global_device_ids=true, to_apply=%region_8.9 | all-reduce | flops 2 | bytes 16 | tf_op jit(solution)/shard_map/psum | solution.py:54
  656.3 1.4 multiply_reduce_fusion.1
  659.6 36.1 %all-gather.18.cloned.1.call-done = f32[128,4096]{1,0:T(8,128)} async-done(((f32[128,512]{1,0:T(8,128)}), f32[128,4096]{1,0:T(8,128)}) %all-gather.18.cloned.1.call-update) | async-done | bytes 2097168 | tf_op jit(solution)/shard_map/all_gather | solution.py:41
  695.7 13.4 %fusion = f32[]{:T(128)} fusion(f32[128,512]{1,0:T(8,128)} %get-tuple-element.13, f32[128,4096]{1,0:T(8,128)} %all-gather.18.cloned.1.call-done, f32[512,4096]{1,0:T(8,128)} %select_add_fusion), kind=kOutput, calls=%fused_computation.5 | convolution fusion | flops 3221356544 | bytes 10747908 | tf_op jit(solution)/shard_map/dot_general | solution.py:40
  709.0 74.2 %all-reduce = (f32[]{:T(128)}, f32[]{:T(128)}) all-reduce(f32[]{:T(128)} %get-tuple-element.12, f32[]{:T(128)} %fusion), channel_id=1, replica_groups=mesh['tok'=16,'col'=8,'grp'=2] {'tok','col','grp'}, use_global_device_ids=true, to_apply=%region_12.13 | all-reduce | flops 2 | bytes 16 | tf_op jit(solution)/shard_map/psum | solution.py:54
  784.8 3.3 fusion.5
  788.1 37.0 %reduce-scatter.5.cloned.1.call-done = f32[256,128]{1,0:T(8,128)} async-done(((f32[2048,128]{1,0:T(8,128)}), f32[256,128]{1,0:T(8,128)}) %reduce-scatter.5.cloned.1.call-update) | async-done | bytes 131088 | tf_op jit(solution)/shard_map/reduce_scatter | solution.py:64
  825.1 1.5 convert_element_type.15
  (44 shorter events, 3.8 us)
Async XLA Ops:
  7.2 80.1 %all-gather.10.cloned.1.call-start = ((), (), s32[]{:S(2)}) async-start(), calls=%async_computation.3 | async-start | bytes 7077888 | tf_op jit(solution)/shard_map/all_gather | solution.py:28
  7.9 232.5 %reduce-scatter.3.cloned.1.call-start = ((), (), s32[]{:S(2)}) async-start(), calls=%async_computation.4 | async-start | bytes 8650752 | tf_op jit(solution)/shard_map/reduce_scatter | solution.py:32
  97.0 143.5 %copy-start.6 = (s32[1,4]{1,0:T(1,128)S(1)}, s32[1,4]{1,0:T(1,128)}, u32[]{:S(2)}) copy-start(s32[1,4]{1,0:T(1,128)} %param.6) | copy-start | bytes 52
  97.0 143.6 %copy-start.4 = (f32[128,512]{1,0:T(8,128)S(1)}, f32[128,512]{1,0:T(8,128)}, u32[]{:S(2)}) copy-start(f32[128,512]{1,0:T(8,128)} %param.5) | copy-start | bytes 786436
  97.0 144.4 %copy-start = (bf16[768,512]{1,0:T(8,128)(2,1)S(1)}, bf16[768,512]{1,0:T(8,128)(2,1)}, u32[]{:S(2)}) copy-start(bf16[768,512]{1,0:T(8,128)(2,1)} %param.4) | copy-start | bytes 2359300
  97.0 246.5 %all-gather.12.cloned.1.call-start = ((), (), s32[]{:S(2)}) async-start(), calls=%async_computation.5 | async-start | bytes 8650752 | tf_op jit(solution)/shard_map/all_gather | solution.py:33
  240.4 146.1 %all-gather.8.cloned.1.call-start = ((), (), s32[]{:S(2)}) async-start(), calls=%async_computation.2 | async-start | bytes 2359296 | tf_op jit(solution)/shard_map/all_gather | solution.py:41
  241.3 198.5 %all-gather.14.cloned.1.call-start = ((), (), s32[]{:S(2)}) async-start(), calls=%async_computation.6 | async-start | bytes 2359296 | tf_op jit(solution)/shard_map/all_gather | solution.py:41
  400.0 167.4 %all-gather.16.cloned.1.call-start = ((), (), s32[]{:S(2)}) async-start(), calls=%async_computation.7 | async-start | bytes 2359296 | tf_op jit(solution)/shard_map/all_gather | solution.py:41
  529.5 128.3 %copy-start.7 = (s32[64]{0:T(128)S(1)}, s32[64]{0:T(128)}, u32[]{:S(2)}) copy-start(s32[64]{0:T(128)} %param.7) | copy-start | bytes 772
  529.5 166.1 %all-gather.18.cloned.1.call-start = ((), (), s32[]{:S(2)}) async-start(), calls=%async_computation.8 | async-start | bytes 2359296 | tf_op jit(solution)/shard_map/all_gather | solution.py:41
  656.3 128.3 %copy-start.1 = (f32[128,512]{1,0:T(8,128)S(1)}, f32[128,512]{1,0:T(8,128)}, u32[]{:S(2)}) copy-start(f32[128,512]{1,0:T(8,128)} %get-tuple-element.14) | copy-start | bytes 786436
  656.3 128.3 %copy-start.3 = (f32[128,512]{1,0:T(8,128)S(1)}, f32[128,512]{1,0:T(8,128)}, u32[]{:S(2)}) copy-start(f32[128,512]{1,0:T(8,128)} %broadcast_multiply_fusion) | copy-start | bytes 786436
  657.7 126.9 %copy-start.2 = (f32[128,512]{1,0:T(8,128)S(1)}, f32[128,512]{1,0:T(8,128)}, u32[]{:S(2)}) copy-start(f32[128,512]{1,0:T(8,128)} %get-tuple-element.13) | copy-start | bytes 786436
  657.8 127.0 %all-gather.20.cloned.1.call-start = ((), (), s32[]{:S(2)}) async-start(), calls=%async_computation.9 | async-start | bytes 2162688 | tf_op jit(solution)/shard_map/all_gather | solution.py:63
  659.3 165.8 %reduce-scatter.5.cloned.1.call-start = ((), (), s32[]{:S(2)}) async-start(), calls=%async_computation.10 | async-start | bytes 1179648 | tf_op jit(solution)/shard_map/reduce_scatter | solution.py:64
  784.8 41.9 %copy-start.5 = (bf16[128,512]{1,0:T(8,128)(2,1)}, bf16[128,512]{1,0:T(8,128)(2,1)S(1)}, u32[]{:S(2)}) copy-start(bf16[128,512]{1,0:T(8,128)(2,1)S(1)} %fusion.3) | copy-start | bytes 393220
Sparse Core Ops, SparseCore 0:
  9.8 77.4 all-gather.9
  97.2 143.1 reduce-scatter.2
  242.1 101.3 all-gather.11
  345.2 41.3 all-gather.7
  400.1 39.6 all-gather.13
  529.7 37.7 all-gather.15
  657.9 37.7 all-gather.17
  698.0 84.5 all-gather.19
  788.3 36.8 reduce-scatter.4
where the time goes:
time: 838 us; the launch traced here: 833 us
  waiting for transfers between devices  433 us (52%)
  blocking collectives  300 us (36%)
  matrix products  66.6 us (8%)
  between operations  18.9 us (2%)
  other arithmetic  12.6 us (2%)
    psum x3, blocking collectives, per_device(): lax.psum((jnp.sum(gradient * gradient), jnp.sum(gradient * image_rows)),...  223 us
    all_gather x4, waiting for transfers between devices, apply_gram(): lax.all_gather(operand, 'col', axis=1, tiled=True)  150 us
    reduce_scatter x1, waiting for transfers between devices, per_device(): lax.psum_scatter(partial_gram, ('tok', 'grp'), scatter_dimension=1, tiled...  143 us
    all_gather x1, waiting for transfers between devices, per_device(): lax.all_gather(calibration, 'col', axis=1, tiled=True)  79.3 us
    psum x1, blocking collectives, per_device(): trace_total = lax.psum(squares, ('tok', 'col', 'grp'))  77.8 us
    dot_general x4, matrix products, apply_gram(): lax.dot_general(lax.all_gather(operand, 'col', axis=1, tiled=True), stati...  53.5 us
    reduce_scatter x1, waiting for transfers between devices, per_device(): lax.psum_scatter(lax.dot_general(all_chosen, new_weight, (((1,), (1,)), (...  37 us
    all_gather x1, waiting for transfers between devices, per_device(): gram_rows = lax.all_gather(gram_slice, ('tok', 'grp'), axis=1, tiled=True)  22.7 us
  transfers between devices with their start and end apart: 9, of which 8 were waited for; matrix products, arithmetic and copies ran while one was open for 3% of the time, Pallas kernels for 0%

commit v1 on v0

--- a/solution.py
+++ b/solution.py
@@ -6,6 +6,18 @@
 TILE = 128
 ITERS = 3
 DAMPING = 0.1
+
+
+def doubled_up(value, axis, dim):
+    ways, here = (lax.axis_size(axis), lax.axis_index(axis))
+    grown, reach = (value, 1)
+    while reach < ways:
+        theirs = lax.ppermute(grown, axis, [(d, d ^ reach) for d in range(ways)])
+        mine_first = jnp.concatenate([grown, theirs], axis=dim)
+        theirs_first = jnp.concatenate([theirs, grown], axis=dim)
+        grown = jnp.where(here & reach == 0, mine_first, theirs_first)
+        reach = 2 * reach
+    return grown
 
 
 def expand_tiles(tile_flags):
@@ -38,7 +50,7 @@
 
     def apply_gram(operand):
         return lax.dot_general(
-            lax.all_gather(operand, "col", axis=1, tiled=True),
+            doubled_up(operand, "col", 1),
             stationary,
             (((1,), (1,)), ((), ())),
             precision=lax.Precision.HIGHEST,

time: 838 us -> 956 us (1.14)
  waiting for transfers between devices: 433 us -> 545 us
  starting transfers between devices: 1.27 us -> 20.4 us
  matrix products: 66.6 us -> 56.6 us
    ppermute x0 -> x12, waiting for transfers between devices: none -> 275 us  [doubled_up(): theirs = lax.ppermute(grown, axis, [(d, d ^ reach) for d in range(ways)])]
    all_gather x4 -> x0, waiting for transfers between devices: 150 us -> none  [apply_gram(): lax.all_gather(operand, 'col', axis=1, tiled=True)]
    ppermute x0 -> x12, starting transfers between devices: none -> 20.1 us  [doubled_up(): theirs = lax.ppermute(grown, axis, [(d, d ^ reach) for d in range(ways)])]
    all_gather x1, waiting for transfers between devices: 22.7 us -> 11.3 us  [per_device(): gram_rows = lax.all_gather(gram_slice, ('tok', 'grp'), axis=1, tiled=True)]
    dot_general x4, matrix products: 53.5 us -> 43.6 us  [apply_gram(): lax.dot_general(doubled_up(operand, 'col', 1), stationary, (((1,), (1,)),...]
  transfers between devices with their start and end apart: 9 -> 17, of which waited for: 8 -> 15; matrix products, arithmetic and copies ran while one was open for 3% -> 4% of each run, Pallas kernels for 0% -> 0%
where the time goes in v1:
time: 956 us; the launch traced here: 950 us
  waiting for transfers between devices  545 us (57%)
  blocking collectives  299 us (31%)
  matrix products  56.6 us (6%)
  starting transfers between devices  20.4 us (2%)
  between operations  18.8 us (2%)
    ppermute x12, waiting for transfers between devices, doubled_up(): theirs = lax.ppermute(grown, axis, [(d, d ^ reach) for d in range(ways)])  275 us
    psum x3, blocking collectives, per_device(): lax.psum((jnp.sum(gradient * gradient), jnp.sum(gradient * image_rows)),...  223 us
    reduce_scatter x1, waiting for transfers between devices, per_device(): lax.psum_scatter(partial_gram, ('tok', 'grp'), scatter_dimension=1, tiled...  143 us
    all_gather x1, waiting for transfers between devices, per_device(): lax.all_gather(calibration, 'col', axis=1, tiled=True)  79.3 us
    psum x1, blocking collectives, per_device(): trace_total = lax.psum(squares, ('tok', 'col', 'grp'))  76.4 us
    dot_general x4, matrix products, apply_gram(): lax.dot_general(doubled_up(operand, 'col', 1), stationary, (((1,), (1,)),...  43.6 us
    reduce_scatter x1, waiting for transfers between devices, per_device(): lax.psum_scatter(lax.dot_general(all_chosen, new_weight, (((1,), (1,)), (...  35.6 us
    ppermute x12, starting transfers between devices, doubled_up(): theirs = lax.ppermute(grown, axis, [(d, d ^ reach) for d in range(ways)])  20.1 us
  transfers between devices with their start and end apart: 17, of which 15 were waited for; matrix products, arithmetic and copies ran while one was open for 4% of the time, Pallas kernels for 0%

profile of v1, /device:TPU:2, one launch (start us, length us, event | category | flops | bytes accessed | tf_op | source)
XLA Modules:
  0.0 950.2 jit_solution(5854952973215173195)
XLA Ops:
  7.9 79.3 %all-gather.4.cloned.1.call-done = bf16[768,4096]{1,0:T(8,128)(2,1)} async-done(((bf16[768,512]{1,0:T(8,128)(2,1)}), bf16[768,4096]{1,0:T(8,128)(2,1)}) %all-gather.4.cloned.1.call-update) | async-done | bytes 6291472 | tf_op jit(solution)/shard_map/all_gather | solution.py:40
  87.3 9.8 %fusion.37 = f32[512,4096]{1,0:T(8,128)} fusion(bf16[768,512]{1,0:T(8,128)(2,1)} %param.4, bf16[768,4096]{1,0:T(8,128)(2,1)} %all-gather.4.cloned.1.call-done), kind=kOutput, calls=%fused_computation.71 | convolution fusion | flops 3221225472 | bytes 15466496 | tf_op jit(solution)/shard_map/dot_general | solution.py:38
  97.1 143.3 %reduce-scatter.3.cloned.1.call-done = f32[512,128]{1,0:T(8,128)} async-done(((f32[512,4096]{1,0:T(8,128)}), f32[512,128]{1,0:T(8,128)}) %reduce-scatter.3.cloned.1.call-update) | async-done | bytes 262160 | tf_op jit(solution)/shard_map/reduce_scatter | solution.py:44
  242.2 6.3 collective-permute-done
  252.2 76.4 %psum.49 = f32[]{:T(128)} all-reduce(f32[]{:T(128)} %multiply_reduce_fusion), channel_id=1, replica_groups=mesh['tok'=16,'col'=8,'grp'=2] {'tok','col','grp'}, use_global_device_ids=true, to_apply=%region_2.0 | all-reduce | flops 1 | bytes 8 | tf_op jit(solution)/shard_map/psum | solution.py:37
  332.3 11.3 %all-gather.6.cloned.1.call-done = f32[512,4096]{1,0:T(8,128)} async-done(((f32[512,128]{1,0:T(8,128)}), f32[512,4096]{1,0:T(8,128)}) %all-gather.6.cloned.1.call-update) | async-done | bytes 8388624 | tf_op jit(solution)/shard_map/all_gather | solution.py:45
  347.9 33.3 %collective-permute-done.2 = f32[128,2048]{1,0:T(8,128)S(1)} collective-permute-done((f32[128,2048]{1,0:T(8,128)S(1)}, f32[128,2048]{1,0:T(8,128)S(1)}, u32[]{:S(2)}, u32[]{:S(2)}) %collective-permute-start.2) | collective-permute-done | bytes 1048608 | tf_op jit(solution)/shard_map/ppermute | solution.py:15
  381.1 8.6 broadcast_multiply_fusion.1
  390.9 7.0 collective-permute-done.3
  398.1 25.0 %collective-permute-done.4 = f32[128,1024]{1,0:T(8,128)S(1)} collective-permute-done((f32[128,1024]{1,0:T(8,128)S(1)}, f32[128,1024]{1,0:T(8,128)S(1)}, u32[]{:S(2)}, u32[]{:S(2)}) %collective-permute-start.4) | collective-permute-done | bytes 524320 | tf_op jit(solution)/shard_map/ppermute | solution.py:15
  424.8 47.6 %collective-permute-done.5 = f32[128,2048]{1,0:T(8,128)S(1)} collective-permute-done((f32[128,2048]{1,0:T(8,128)S(1)}, f32[128,2048]{1,0:T(8,128)S(1)}, u32[]{:S(2)}, u32[]{:S(2)}) %collective-permute-start.5) | collective-permute-done | bytes 1048608 | tf_op jit(solution)/shard_map/ppermute | solution.py:15
  472.4 9.2 multiply_reduce_fusion.4
  481.5 73.9 %all-reduce.2 = (f32[]{:T(128)}, f32[]{:T(128)}) all-reduce(f32[]{:T(128)} %get-tuple-element.5, f32[]{:T(128)} %get-tuple-element.4), channel_id=1, replica_groups=mesh['tok'=16,'col'=8,'grp'=2] {'tok','col','grp'}, use_global_device_ids=true, to_apply=%region_4.5 | all-reduce | flops 2 | bytes 16 | tf_op jit(solution)/shard_map/psum | solution.py:66
  558.6 6.4 collective-permute-done.6
  566.1 23.9 %collective-permute-done.7 = f32[128,1024]{1,0:T(8,128)S(1)} collective-permute-done((f32[128,1024]{1,0:T(8,128)S(1)}, f32[128,1024]{1,0:T(8,128)S(1)}, u32[]{:S(2)}, u32[]{:S(2)}) %collective-permute-start.7) | collective-permute-done | bytes 524320 | tf_op jit(solution)/shard_map/ppermute | solution.py:15
  595.2 45.4 %collective-permute-done.8 = f32[128,2048]{1,0:T(8,128)} collective-permute-done((f32[128,2048]{1,0:T(8,128)S(1)}, f32[128,2048]{1,0:T(8,128)}, u32[]{:S(2)}, u32[]{:S(2)}) %collective-permute-start.8) | collective-permute-done | bytes 1048608 | tf_op jit(solution)/shard_map/ppermute | solution.py:15
  640.6 13.3 %multiply_reduce_fusion.2 = (f32[]{:T(128)}, f32[]{:T(128)}, f32[128,512]{1,0:T(8,128)S(1)}) fusion(f32[128,512]{1,0:T(8,128)S(1)} %broadcast_multiply_fusion, f32[512,4096]{1,0:T(8,128)} %copy-done, f32[128,2048]{1,0:T(8,128)} %collective-permute-done.8, f32[128,2048]{1,0:T(8,128)S(1)} %maximum_select_fusion.12, pred[]{:T(512)S(6)} %eq.8), kind=kOutput, calls=%fused_computation.53 | convolution fusion | flops 3223060480 | bytes 11010057 | tf_op jit(solution)/shard_map/dot_general | solution.py:52
  653.9 75.1 %all-reduce.1 = (f32[]{:T(128)}, f32[]{:T(128)}) all-reduce(f32[]{:T(128)} %get-tuple-element.3, f32[]{:T(128)} %get-tuple-element.2), channel_id=1, replica_groups=mesh['tok'=16,'col'=8,'grp'=2] {'tok','col','grp'}, use_global_device_ids=true, to_apply=%region_8.9 | all-reduce | flops 2 | bytes 16 | tf_op jit(solution)/shard_map/psum | solution.py:66
  731.6 7.4 collective-permute-done.9
  739.4 24.7 %collective-permute-done.10 = f32[128,1024]{1,0:T(8,128)S(1)} collective-permute-done((f32[128,1024]{1,0:T(8,128)S(1)}, f32[128,1024]{1,0:T(8,128)S(1)}, u32[]{:S(2)}, u32[]{:S(2)}) %collective-permute-start.10) | collective-permute-done | bytes 524320 | tf_op jit(solution)/shard_map/ppermute | solution.py:15
  767.3 48.1 %collective-permute-done.11 = f32[128,2048]{1,0:T(8,128)S(1)} collective-permute-done((f32[128,2048]{1,0:T(8,128)S(1)}, f32[128,2048]{1,0:T(8,128)S(1)}, u32[]{:S(2)}, u32[]{:S(2)}) %collective-permute-start.11) | collective-permute-done | bytes 1048608 | tf_op jit(solution)/shard_map/ppermute | solution.py:15
  815.4 12.5 %fusion.29 = f32[]{:T(128)} fusion(f32[128,512]{1,0:T(8,128)S(1)} %get-tuple-element.13, f32[512,4096]{1,0:T(8,128)} %copy-done, f32[128,2048]{1,0:T(8,128)S(1)} %collective-permute-done.11, f32[128,2048]{1,0:T(8,128)S(1)} %maximum_select_fusion.13, pred[]{:T(512)S(6)} %eq.8), kind=kOutput, calls=%fused_computation.41 | convolution fusion | flops 3222929408 | bytes 10747909 | tf_op jit(solution)/shard_map/dot_general | solution.py:52
  827.9 73.5 %all-reduce = (f32[]{:T(128)}, f32[]{:T(128)}) all-reduce(f32[]{:T(128)} %get-tuple-element.12, f32[]{:T(128)} %fusion.29), channel_id=1, replica_groups=mesh['tok'=16,'col'=8,'grp'=2] {'tok','col','grp'}, use_global_device_ids=true, to_apply=%region_12.13 | all-reduce | flops 2 | bytes 16 | tf_op jit(solution)/shard_map/psum | solution.py:66
  906.3 35.6 %reduce-scatter.5.cloned.1.call-done = f32[256,128]{1,0:T(8,128)} async-done(((f32[2048,128]{1,0:T(8,128)}), f32[256,128]{1,0:T(8,128)}) %reduce-scatter.5.cloned.1.call-update) | async-done | bytes 131088 | tf_op jit(solution)/shard_map/reduce_scatter | solution.py:76
  (62 shorter events, 34.6 us)
Async XLA Ops:
  7.2 80.1 %all-gather.4.cloned.1.call-start = ((), (), s32[]{:S(2)}) async-start(), calls=%async_computation.2 | async-start | bytes 7077888 | tf_op jit(solution)/shard_map/all_gather | solution.py:40
  7.9 232.5 %reduce-scatter.3.cloned.1.call-start = ((), (), s32[]{:S(2)}) async-start(), calls=%async_computation.3 | async-start | bytes 8650752 | tf_op jit(solution)/shard_map/reduce_scatter | solution.py:44
  97.0 143.5 %copy-start.5 = (s32[1,4]{1,0:T(1,128)S(1)}, s32[1,4]{1,0:T(1,128)}, u32[]{:S(2)}) copy-start(s32[1,4]{1,0:T(1,128)} %param.6) | copy-start | bytes 52
  97.0 143.5 %copy-start.2 = (f32[128,512]{1,0:T(8,128)S(1)}, f32[128,512]{1,0:T(8,128)}, u32[]{:S(2)}) copy-start(f32[128,512]{1,0:T(8,128)} %param.5) | copy-start | bytes 786436
  97.0 154.1 %copy-start.1 = (bf16[768,512]{1,0:T(8,128)(2,1)S(1)}, bf16[768,512]{1,0:T(8,128)(2,1)}, u32[]{:S(2)}) copy-start(bf16[768,512]{1,0:T(8,128)(2,1)} %param.4) | copy-start | bytes 2359300
  97.0 246.5 %all-gather.6.cloned.1.call-start = ((), (), s32[]{:S(2)}) async-start(), calls=%async_computation.4 | async-start | bytes 8650752 | tf_op jit(solution)/shard_map/all_gather | solution.py:45
  240.4 662.5 %all-gather.8.cloned.1.call-start = ((), (), s32[]{:S(2)}) async-start(), calls=%async_computation.5 | async-start | bytes 2162688 | tf_op jit(solution)/shard_map/all_gather | solution.py:75
  240.6 7.9 collective-permute-start
  248.5 80.7 %collective-permute-start.1 = (f32[128,1024]{1,0:T(8,128)S(1)}, f32[128,1024]{1,0:T(8,128)S(1)}, u32[]{:S(2)}, u32[]{:S(2)}) collective-permute-start(f32[128,1024]{1,0:T(8,128)S(1)} %maximum_select_fusion.16), channel_id=1, source_target_pairs={{0,4},{2,6},{4,0},{6,2},{8,12},{10,14},{12,8},{14,10},{1,5},{3,7},... | collective-permute-start | bytes 1572872 | tf_op jit(solution)/shard_map/ppermute | solution.py:15
  329.5 51.7 %collective-permute-start.2 = (f32[128,2048]{1,0:T(8,128)S(1)}, f32[128,2048]{1,0:T(8,128)S(1)}, u32[]{:S(2)}, u32[]{:S(2)}) collective-permute-start(f32[128,2048]{1,0:T(8,128)S(1)} %maximum_select_fusion.10), channel_id=1, source_target_pairs={{0,8},{2,10},{4,12},{6,14},{8,0},{10,2},{12,4},{14,6},{1,9},{3,11}... | collective-permute-start | bytes 3145736 | tf_op jit(solution)/shard_map/ppermute | solution.py:15
  347.9 124.5 %copy-start = (f32[512,4096]{1,0:T(8,128)}, f32[512,4096]{1,0:T(8,128)S(1)}, u32[]{:S(2)}) copy-start(f32[512,4096]{1,0:T(8,128)S(1)} %select_add_fusion) | copy-start | bytes 25165828
  389.7 8.2 collective-permute-start.3
  398.0 25.1 %collective-permute-start.4 = (f32[128,1024]{1,0:T(8,128)S(1)}, f32[128,1024]{1,0:T(8,128)S(1)}, u32[]{:S(2)}, u32[]{:S(2)}) collective-permute-start(f32[128,1024]{1,0:T(8,128)S(1)} %maximum_select_fusion.17), channel_id=1, source_target_pairs={{0,4},{2,6},{4,0},{6,2},{8,12},{10,14},{12,8},{14,10},{1,5},{3,7},... | collective-permute-start | bytes 1572872 | tf_op jit(solution)/shard_map/ppermute | solution.py:15
  423.2 49.1 %collective-permute-start.5 = (f32[128,2048]{1,0:T(8,128)S(1)}, f32[128,2048]{1,0:T(8,128)S(1)}, u32[]{:S(2)}, u32[]{:S(2)}) collective-permute-start(f32[128,2048]{1,0:T(8,128)S(1)} %maximum_select_fusion.11), channel_id=1, source_target_pairs={{0,8},{2,10},{4,12},{6,14},{8,0},{10,2},{12,4},{14,6},{1,9},{3,11}... | collective-permute-start | bytes 3145736 | tf_op jit(solution)/shard_map/ppermute | solution.py:15
  481.5 112.0 %copy-start.6 = (s32[64]{0:T(128)S(1)}, s32[64]{0:T(128)}, u32[]{:S(2)}) copy-start(s32[64]{0:T(128)} %param.7) | copy-start | bytes 772
  556.9 8.1 collective-permute-start.6
  565.0 25.0 %collective-permute-start.7 = (f32[128,1024]{1,0:T(8,128)S(1)}, f32[128,1024]{1,0:T(8,128)S(1)}, u32[]{:S(2)}, u32[]{:S(2)}) collective-permute-start(f32[128,1024]{1,0:T(8,128)S(1)} %maximum_select_fusion.18), channel_id=1, source_target_pairs={{0,4},{2,6},{4,0},{6,2},{8,12},{10,14},{12,8},{14,10},{1,5},{3,7},... | collective-permute-start | bytes 1572872 | tf_op jit(solution)/shard_map/ppermute | solution.py:15
  590.2 50.4 %collective-permute-start.8 = (f32[128,2048]{1,0:T(8,128)S(1)}, f32[128,2048]{1,0:T(8,128)}, u32[]{:S(2)}, u32[]{:S(2)}) collective-permute-start(f32[128,2048]{1,0:T(8,128)S(1)} %maximum_select_fusion.12), channel_id=1, source_target_pairs={{0,8},{2,10},{4,12},{6,14},{8,0},{10,2},{12,4},{14,6},{1,9},{3,11}... | collective-permute-start | bytes 3145736 | tf_op jit(solution)/shard_map/ppermute | solution.py:15
  595.0 346.9 %reduce-scatter.5.cloned.1.call-start = ((), (), s32[]{:S(2)}) async-start(), calls=%async_computation.6 | async-start | bytes 1179648 | tf_op jit(solution)/shard_map/reduce_scatter | solution.py:76
  731.0 8.0 collective-permute-start.9
  739.1 25.0 %collective-permute-start.10 = (f32[128,1024]{1,0:T(8,128)S(1)}, f32[128,1024]{1,0:T(8,128)S(1)}, u32[]{:S(2)}, u32[]{:S(2)}) collective-permute-start(f32[128,1024]{1,0:T(8,128)S(1)} %maximum_select_fusion.19), channel_id=1, source_target_pairs={{0,4},{2,6},{4,0},{6,2},{8,12},{10,14},{12,8},{14,10},{1,5},{3,7},... | collective-permute-start | bytes 1572872 | tf_op jit(solution)/shard_map/ppermute | solution.py:15
  764.2 138.5 %copy-start.3 = (f32[128,512]{1,0:T(8,128)S(1)}, f32[128,512]{1,0:T(8,128)}, u32[]{:S(2)}) copy-start(f32[128,512]{1,0:T(8,128)} %param.5) | copy-start | bytes 786436
  764.2 51.1 %collective-permute-start.11 = (f32[128,2048]{1,0:T(8,128)S(1)}, f32[128,2048]{1,0:T(8,128)S(1)}, u32[]{:S(2)}, u32[]{:S(2)}) collective-permute-start(f32[128,2048]{1,0:T(8,128)S(1)} %maximum_select_fusion.13), channel_id=1, source_target_pairs={{0,8},{2,10},{4,12},{6,14},{8,0},{10,2},{12,4},{14,6},{1,9},{3,11}... | collective-permute-start | bytes 3145736 | tf_op jit(solution)/shard_map/ppermute | solution.py:15
  902.9 3.4 copy-start.4
Sparse Core Ops, SparseCore 0:
  9.8 77.4 all-gather.3
  97.2 143.1 reduce-scatter.2
  242.1 101.4 all-gather.5
  595.1 82.8 all-gather.7
  906.4 35.4 reduce-scatter.4
